TPU v7x, 256 devices: a whole 4x4x8 slice. The times are simulated.
256 devices in a mesh: ctx: 32 (over z, y_hi, core), ch: 8 (over y_lo, x).
Axes of the slice: x: 4, y: 4 (y_hi: 2, y_lo: 2; y = y_hi * 2 + y_lo), z: 8, core: 2. Of those that a mesh axis runs over, the one named last changes fastest.
Arguments:
- query: bfloat16 [16384, 4096], P('ctx', 'ch'), may hold values from -6 to 6
- keys: bfloat16 [16384, 4096], P('ctx', 'ch'), may hold values from -6 to 6
- values: bfloat16 [16384, 4096], P('ctx', 'ch'), may hold values from -6 to 6
- filters: bfloat16 [2048, 4096], P(None, 'ch'), may hold values from -0.125 to 0.125
- segment_ids: int32 [32], P('ctx'), may hold values from 0 to 15, never falling along the last dimension, each value on 1 to 8 neighbouring positions
- out_weight: bfloat16 [4096, 4096], P('ch'), may hold values from -0.125 to 0.125
Outputs:
- mixed_out: bfloat16 [16384, 4096], P('ctx', 'ch')
Inputs may be any that keep to these rules, and one draw needn't show every extreme that they name: `segment_ids`: document ids never fall along the sequence; a document covers 1 to 8 whole blocks.
All inputs are finite; a program needn't handle non-finite values.
Results may differ from a plain program's by a relative error of at most 0.024.
Values may be sent and summed in bfloat16 or wider, within the bound.
A program may use at most 128 MiB of HBM per device.

v0:
```python
import math

import jax
import jax.numpy as jnp
from jax import lax
from jax.sharding import PartitionSpec as P


def passed_along(value, axis, steps):
    count = lax.axis_size(axis)
    initial, last = (max(0, -steps), min(count, count - steps))
    return lax.ppermute(value, axis, [(source, source + steps) for source in range(initial, last)])


def tables(block_len):
    period = 2 * block_len
    frequency = jnp.arange(period, dtype=jnp.int32)[:, None]
    position = jnp.arange(block_len, dtype=jnp.int32)[None, :]
    angles = 2.0 * math.pi / period * (frequency * position % period).astype(jnp.float32)
    forward = jnp.concatenate([jnp.cos(angles), -jnp.sin(angles)], 0).astype(jnp.bfloat16)
    out_rows = jnp.arange(block_len, dtype=jnp.int32)[:, None] + block_len
    freq_cols = jnp.arange(period, dtype=jnp.int32)[None, :]
    angles_back = 2.0 * math.pi / period * (out_rows * freq_cols % period).astype(jnp.float32)
    backward = (jnp.concatenate([jnp.cos(angles_back), -jnp.sin(angles_back)], 1) / period).astype(
        jnp.bfloat16
    )
    return (forward, backward)


def segment_kernels(filters, forward, block_len, reach_blocks):
    period = 2 * block_len
    parity = (1 - 2 * (jnp.arange(period, dtype=jnp.int32) % 2)).astype(jnp.float32)
    parity = jnp.concatenate([parity, parity])[:, None]
    halves = [
        jnp.dot(
            forward,
            filters[offset * block_len : (offset + 1) * block_len],
            preferred_element_type=jnp.float32,
        )
        for offset in range(reach_blocks)
    ]
    kernels = []
    for offset in range(reach_blocks + 1):
        current = parity * halves[offset] if offset < reach_blocks else 0.0
        previous = halves[offset - 1] if offset > 0 else 0.0
        kernels.append(previous + current)
    return kernels


def complex_product(spectrum, kernel):
    period = spectrum.shape[0] // 2
    spec_f = spectrum.astype(jnp.float32)
    real_in, imag_in = (spec_f[:period], spec_f[period:])
    real_kern, imag_kern = (kernel[:period], kernel[period:])
    return jnp.concatenate(
        [real_in * real_kern - imag_in * imag_kern, real_in * imag_kern + imag_in * real_kern], 0
    )


def on_device(query, keys, values, filters, segment_ids, out_weight):
    block_len = query.shape[0]
    reach_blocks = filters.shape[0] // block_len
    forward, backward = tables(block_len)
    kernels = segment_kernels(filters, forward, block_len, reach_blocks)
    mixed_in = (keys.astype(jnp.float32) * values.astype(jnp.float32)).astype(jnp.bfloat16)
    own_spectrum = jnp.dot(forward, mixed_in, preferred_element_type=jnp.float32).astype(
        jnp.bfloat16
    )
    position = lax.axis_index("ctx")
    own_segment = segment_ids[0]
    accumulated = complex_product(own_spectrum, kernels[0])
    moving = (mixed_in, segment_ids)
    for offset in range(1, reach_blocks + 1):
        moving = passed_along((moving[0], moving[1]), "ctx", 1)
        allowed = jnp.logical_and(position - offset >= 0, moving[1][0] == own_segment)
        product = complex_product(
            jnp.dot(forward, moving[0], preferred_element_type=jnp.float32).astype(jnp.bfloat16),
            kernels[offset],
        )
        accumulated = accumulated + jnp.where(allowed, product, jnp.zeros_like(product))
    filtered = jnp.dot(
        backward, accumulated.astype(jnp.bfloat16), preferred_element_type=jnp.float32
    )
    gated_rows = (query.astype(jnp.float32) * filtered).astype(jnp.bfloat16)
    partial_sums = jnp.dot(gated_rows, out_weight, preferred_element_type=jnp.float32)
    return lax.psum_scatter(
        partial_sums.astype(jnp.bfloat16), "ch", scatter_dimension=1, tiled=True
    )


def solution(mesh):
    in_specs = (
        P("ctx", "ch"),
        P("ctx", "ch"),
        P("ctx", "ch"),
        P(None, "ch"),
        P("ctx"),
        P("ch", None),
    )
    out_specs = P("ctx", "ch")
    return jax.shard_map(
        on_device, mesh=mesh, in_specs=in_specs, out_specs=out_specs, check_vma=False
    )
```

profile of v0, /device:TPU:128, one launch (start us, length us, event | category | flops | bytes accessed | tf_op | source)
XLA Modules:
  0.0 209.2 jit_solution(11358772212696154438)
XLA Ops:
  6.5 0.0 reduce-scatter.2.cloned.1.call-start
  6.5 0.0 copy-start.10
  6.5 1.5 multiply_convert_fusion.1
  8.0 1.9 collective-permute-start.1
  10.0 5.2 %collective-permute-start = (s32[1]{0:T(128)}, s32[1]{0:T(128)}, u32[]{:S(2)}, u32[]{:S(2)}) collective-permute-start(s32[1]{0:T(128)} %param.10), channel_id=1, source_target_pairs={{0,8},{8,16},{16,24},{24,32},{32,40},{40,48},{48,56},{56,64},{64,7... | collective-permute-start | bytes 20 | tf_op jit(solution)/shard_map/ppermute | solution.py:12
  15.2 8.5 %negate_convert_fusion = (bf16[1024,512]{1,0:T(8,128)(2,1)S(1)}, bf16[1024,512]{1,0:T(8,128)(2,1)S(1)}) fusion(), kind=kLoop, calls=%fused_computation.50 | loop fusion | flops 8912896 | bytes 2097152 | tf_op jit(solution)/shard_map/convert.1
  23.7 0.0 copy-done.10
  23.7 1.2 fusion.31
  25.0 0.0 copy-start
  25.0 1.3 fusion.35
  26.3 1.3 fusion.37
  27.5 10.6 %fusion.26 = (f32[512,1024]{1,0:T(8,128)}, f32[512,1024]{1,0:T(8,128)}) fusion(s32[512]{0:T(512)S(1)} %iota_add_fusion), kind=kLoop, calls=%fused_computation.62 | loop fusion | flops 7864320 | bytes 4196352 | tf_op jit(solution)/shard_map/cos | solution.py:24
  38.2 0.0 copy-done
  38.2 7.7 %multiply_add_fusion = (f32[2048,512]{1,0:T(8,128)}, f32[2048,512]{1,0:T(8,128)}, f32[2048,512]{1,0:T(8,128)}, f32[2048,512]{1,0:T(8,128)}) fusion(f32[2048,512]{1,0:T(8,128)S(1)} %fusion.31, f32[2048]{0:T(1024)S(1)} %pad_maximum_fusion.1, f32[2048,512]{1,0:T(8,128)S(1)} %fusion.35, f32[2048,512]{1,0:T(8,128)S(1)} %fusion.37, ...), kind=kOutput, calls=%fused_computation.12 | convolution fusion | flops 1085276160 | bytes 31989760 | tf_op jit(solution)/shard_map/dot_general | solution.py:35
  45.9 3.3 %fusion.9 = f32[2048,512]{1,0:T(8,128)} fusion(bf16[512,512]{1,0:T(8,128)(2,1)S(1)} %multiply_convert_fusion.1, bf16[1024,512]{1,0:T(8,128)(2,1)S(1)} %get-tuple-element.21, bf16[1024,512]{1,0:T(8,128)(2,1)S(1)} %get-tuple-element.22), kind=kOutput, calls=%fused_computation.30 | convolution fusion | flops 1080033280 | bytes 6815744 | tf_op jit(solution)/shard_map/dot_general | solution.py:66
  49.8 6.7 %multiply_subtract_fusion.4 = (f32[1024,512]{1,0:T(8,128)}, f32[1024,512]{1,0:T(8,128)}) fusion(f32[2048,512]{1,0:T(8,128)} %get-tuple-element.18, f32[2048,512]{1,0:T(8,128)} %fusion.9), kind=kLoop, calls=%fused_computation.48 | loop fusion | flops 3145728 | bytes 12582912 | tf_op jit(solution)/shard_map/sub | solution.py:56
  56.5 0.0 collective-permute-done
  57.2 1.9 collective-permute-start.2
  59.1 6.9 %collective-permute-done.2 = s32[1]{0:T(128)} collective-permute-done((s32[1]{0:T(128)}, s32[1]{0:T(128)}, u32[]{:S(2)}, u32[]{:S(2)}) %collective-permute-start.2) | collective-permute-done | bytes 36 | tf_op jit(solution)/shard_map/ppermute | solution.py:12
  66.6 1.9 collective-permute-start.4
  68.5 6.6 %collective-permute-done.4 = s32[1]{0:T(128)} collective-permute-done((s32[1]{0:T(128)}, s32[1]{0:T(128)}, u32[]{:S(2)}, u32[]{:S(2)}) %collective-permute-start.4) | collective-permute-done | bytes 36 | tf_op jit(solution)/shard_map/ppermute | solution.py:12
  75.7 1.9 collective-permute-start.6
  77.6 6.9 %collective-permute-done.6 = s32[1]{0:T(128)} collective-permute-done((s32[1]{0:T(128)}, s32[1]{0:T(128)}, u32[]{:S(2)}, u32[]{:S(2)}) %collective-permute-start.6) | collective-permute-done | bytes 36 | tf_op jit(solution)/shard_map/ppermute | solution.py:12
  85.0 0.0 collective-permute-done.1
  85.1 1.9 collective-permute-start.3
  87.0 0.0 copy-start.4
  87.0 1.3 fusion.8
  88.3 0.9 copy-done.4
  89.2 2.3 %multiply_subtract_fusion.3 = (f32[1024,512]{1,0:T(8,128)S(1)}, f32[1024,512]{1,0:T(8,128)}) fusion(f32[2048,512]{1,0:T(8,128)S(1)} %copy-done.4, f32[2048,512]{1,0:T(8,128)S(1)} %fusion.8), kind=kLoop, calls=%fused_computation.46 | loop fusion | flops 3145728 | bytes 12582912 | tf_op jit(solution)/shard_map/sub | solution.py:56
  91.5 7.7 %collective-permute-done.3 = bf16[512,512]{1,0:T(8,128)(2,1)S(1)} collective-permute-done((bf16[512,512]{1,0:T(8,128)(2,1)S(1)}, bf16[512,512]{1,0:T(8,128)(2,1)S(1)}, u32[]{:S(2)}, u32[]{:S(2)}) %collective-permute-start.3) | collective-permute-done | bytes 524320 | tf_op jit(solution)/shard_map/ppermute | solution.py:12
  99.2 2.1 collective-permute-start.5
  101.3 0.0 copy-start.3
  101.3 1.2 fusion.7
  102.5 0.9 copy-done.3
  103.5 3.0 %multiply_subtract_fusion.2 = (f32[1024,512]{1,0:T(8,128)}, f32[1024,512]{1,0:T(8,128)}) fusion(f32[2048,512]{1,0:T(8,128)S(1)} %copy-done.3, f32[2048,512]{1,0:T(8,128)S(1)} %fusion.7), kind=kLoop, calls=%fused_computation.44 | loop fusion | flops 3145728 | bytes 12582912 | tf_op jit(solution)/shard_map/sub | solution.py:56
  106.5 6.8 %collective-permute-done.5 = bf16[512,512]{1,0:T(8,128)(2,1)S(1)} collective-permute-done((bf16[512,512]{1,0:T(8,128)(2,1)S(1)}, bf16[512,512]{1,0:T(8,128)(2,1)S(1)}, u32[]{:S(2)}, u32[]{:S(2)}) %collective-permute-start.5) | collective-permute-done | bytes 524320 | tf_op jit(solution)/shard_map/ppermute | solution.py:12
  113.3 1.9 collective-permute-start.7
  115.2 0.0 copy-start.2
  115.2 1.2 fusion.6
  116.5 0.9 copy-done.2
  117.4 3.1 %multiply_subtract_fusion.1 = (f32[1024,512]{1,0:T(8,128)}, f32[1024,512]{1,0:T(8,128)}) fusion(f32[2048,512]{1,0:T(8,128)S(1)} %copy-done.2, f32[2048,512]{1,0:T(8,128)S(1)} %fusion.6), kind=kLoop, calls=%fused_computation.42 | loop fusion | flops 3145728 | bytes 12582912 | tf_op jit(solution)/shard_map/sub | solution.py:56
  120.5 6.9 %collective-permute-done.7 = bf16[512,512]{1,0:T(8,128)(2,1)S(1)} collective-permute-done((bf16[512,512]{1,0:T(8,128)(2,1)S(1)}, bf16[512,512]{1,0:T(8,128)(2,1)S(1)}, u32[]{:S(2)}, u32[]{:S(2)}) %collective-permute-start.7) | collective-permute-done | bytes 524320 | tf_op jit(solution)/shard_map/ppermute | solution.py:12
  127.4 0.0 copy-start.1
  127.4 1.2 fusion.5
  128.6 0.9 copy-done.1
  129.6 0.0 copy-start.5
  129.6 0.0 copy-start.6
  129.6 0.0 copy-start.7
  129.6 0.0 copy-start.8
  129.6 0.0 copy-start.9
  129.6 0.0 copy-start.11
  129.6 3.2 %multiply_subtract_fusion = (f32[1024,512]{1,0:T(8,128)}, f32[1024,512]{1,0:T(8,128)}) fusion(f32[2048,512]{1,0:T(8,128)S(1)} %copy-done.1, f32[2048,512]{1,0:T(8,128)S(1)} %fusion.5), kind=kLoop, calls=%fused_computation.40 | loop fusion | flops 3145728 | bytes 12582912 | tf_op jit(solution)/shard_map/sub | solution.py:56
  132.8 0.0 copy-done.5
  132.8 0.0 copy-done.6
  132.8 1.1 copy-done.7
  133.9 0.6 copy-done.8
  134.5 0.6 copy-done.9
  135.1 0.0 copy-done.11
  135.2 5.9 %multiply_convert_fusion = bf16[512,512]{1,0:T(8,128)(2,1)S(1)} fusion(bf16[512,512]{1,0:T(8,128)(2,1)S(1)} %copy-done.11, f32[1024,512]{1,0:T(8,128)S(1)} %copy-done.8, f32[1024,512]{1,0:T(8,128)S(1)} %copy-done.7, f32[1024,512]{1,0:T(8,128)S(1)} %copy-done.9, f32[1024,512]{1,0:T(8,128)S(1)} %get-tuple-element.11, f32[1024,512]{1,0:T(8,128)} %get-tuple-element.10, ...), kind=kOutput, calls=%fused_computation.60 | convolution fusion | flops 1092354048 | bytes 26214404 | tf_op jit(solution)/shard_map/dot_general | solution.py:81
  141.1 6.5 %convolution_convert_fusion = bf16[512,4096]{1,0:T(8,128)(2,1)} fusion(bf16[512,512]{1,0:T(8,128)(2,1)S(1)} %multiply_convert_fusion, bf16[512,4096]{1,0:T(8,128)(2,1)} %param.11), kind=kOutput, calls=%fused_computation | convolution fusion | flops 2149580800 | bytes 8912896 | tf_op jit(solution)/shard_map/dot_general | solution.py:85
  147.6 0.0 reduce-scatter.2.cloned.1.call-update
  147.6 54.8 %reduce-scatter.2.cloned.1.call-done = bf16[512,512]{1,0:T(8,128)(2,1)} async-done(((bf16[512,4096]{1,0:T(8,128)(2,1)}), bf16[512,512]{1,0:T(8,128)(2,1)}) %reduce-scatter.2.cloned.1.call-update) | async-done | bytes 524304 | tf_op jit(solution)/shard_map/reduce_scatter | solution.py:86
  (3 shorter events, 0.0 us)
Async XLA Ops:
  6.5 195.8 %reduce-scatter.2.cloned.1.call-start = ((), (), s32[]{:S(2)}) async-start(), calls=%async_computation.1 | async-start | bytes 4718592 | tf_op jit(solution)/shard_map/reduce_scatter | solution.py:86
  6.5 17.2 %copy-start.10 = (bf16[2048,512]{1,0:T(8,128)(2,1)S(1)}, bf16[2048,512]{1,0:T(8,128)(2,1)}, u32[]{:S(2)}) copy-start(bf16[2048,512]{1,0:T(8,128)(2,1)} %param.9) | copy-start | bytes 6291460
  8.0 77.0 %collective-permute-start.1 = (bf16[512,512]{1,0:T(8,128)(2,1)S(1)}, bf16[512,512]{1,0:T(8,128)(2,1)S(1)}, u32[]{:S(2)}, u32[]{:S(2)}) collective-permute-start(bf16[512,512]{1,0:T(8,128)(2,1)S(1)} %multiply_convert_fusion.1), channel_id=1, source_target_pairs={{0,8},{8,16},{16,24},{24,32},{32,40},{40,48},{48,56},{56,64},{64,7... | collective-permute-start | bytes 1572872 | tf_op jit(solution)/shard_map/ppermute | solution.py:12
  10.0 46.5 %collective-permute-start = (s32[1]{0:T(128)}, s32[1]{0:T(128)}, u32[]{:S(2)}, u32[]{:S(2)}) collective-permute-start(s32[1]{0:T(128)} %param.10), channel_id=1, source_target_pairs={{0,8},{8,16},{16,24},{24,32},{32,40},{40,48},{48,56},{56,64},{64,7... | collective-permute-start | bytes 20 | tf_op jit(solution)/shard_map/ppermute | solution.py:12
  25.0 13.2 %copy-start = (f32[2048,512]{1,0:T(8,128)}, f32[2048,512]{1,0:T(8,128)S(1)}, u32[]{:S(2)}) copy-start(f32[2048,512]{1,0:T(8,128)S(1)} %fusion.31) | copy-start | bytes 12582916
  57.2 8.8 %collective-permute-start.2 = (s32[1]{0:T(128)}, s32[1]{0:T(128)}, u32[]{:S(2)}, u32[]{:S(2)}) collective-permute-start(s32[1]{0:T(128)} %collective-permute-done), channel_id=1, source_target_pairs={{0,8},{8,16},{16,24},{24,32},{32,40},{40,48},{48,56},{56,64},{64,7... | collective-permute-start | bytes 20 | tf_op jit(solution)/shard_map/ppermute | solution.py:12
  66.6 8.5 %collective-permute-start.4 = (s32[1]{0:T(128)}, s32[1]{0:T(128)}, u32[]{:S(2)}, u32[]{:S(2)}) collective-permute-start(s32[1]{0:T(128)} %collective-permute-done.2), channel_id=1, source_target_pairs={{0,8},{8,16},{16,24},{24,32},{32,40},{40,48},{48,56},{56,64},{64,7... | collective-permute-start | bytes 20 | tf_op jit(solution)/shard_map/ppermute | solution.py:12
  75.7 8.8 %collective-permute-start.6 = (s32[1]{0:T(128)}, s32[1]{0:T(128)}, u32[]{:S(2)}, u32[]{:S(2)}) collective-permute-start(s32[1]{0:T(128)} %collective-permute-done.4), channel_id=1, source_target_pairs={{0,8},{8,16},{16,24},{24,32},{32,40},{40,48},{48,56},{56,64},{64,7... | collective-permute-start | bytes 20 | tf_op jit(solution)/shard_map/ppermute | solution.py:12
  85.1 14.1 %collective-permute-start.3 = (bf16[512,512]{1,0:T(8,128)(2,1)S(1)}, bf16[512,512]{1,0:T(8,128)(2,1)S(1)}, u32[]{:S(2)}, u32[]{:S(2)}) collective-permute-start(bf16[512,512]{1,0:T(8,128)(2,1)S(1)} %collective-permute-done.1), channel_id=1, source_target_pairs={{0,8},{8,16},{16,24},{24,32},{32,40},{40,48},{48,56},{56,64},{64,7... | collective-permute-start | bytes 1572872 | tf_op jit(solution)/shard_map/ppermute | solution.py:12
  87.0 2.2 %copy-start.4 = (f32[2048,512]{1,0:T(8,128)S(1)}, f32[2048,512]{1,0:T(8,128)}, u32[]{:S(2)}) copy-start(f32[2048,512]{1,0:T(8,128)} %get-tuple-element.17) | copy-start | bytes 12582916
  99.2 14.1 %collective-permute-start.5 = (bf16[512,512]{1,0:T(8,128)(2,1)S(1)}, bf16[512,512]{1,0:T(8,128)(2,1)S(1)}, u32[]{:S(2)}, u32[]{:S(2)}) collective-permute-start(bf16[512,512]{1,0:T(8,128)(2,1)S(1)} %collective-permute-done.3), channel_id=1, source_target_pairs={{0,8},{8,16},{16,24},{24,32},{32,40},{40,48},{48,56},{56,64},{64,7... | collective-permute-start | bytes 1572872 | tf_op jit(solution)/shard_map/ppermute | solution.py:12
  101.3 2.2 %copy-start.3 = (f32[2048,512]{1,0:T(8,128)S(1)}, f32[2048,512]{1,0:T(8,128)}, u32[]{:S(2)}) copy-start(f32[2048,512]{1,0:T(8,128)} %get-tuple-element.16) | copy-start | bytes 12582916
  113.3 14.1 %collective-permute-start.7 = (bf16[512,512]{1,0:T(8,128)(2,1)S(1)}, bf16[512,512]{1,0:T(8,128)(2,1)S(1)}, u32[]{:S(2)}, u32[]{:S(2)}) collective-permute-start(bf16[512,512]{1,0:T(8,128)(2,1)S(1)} %collective-permute-done.5), channel_id=1, source_target_pairs={{0,8},{8,16},{16,24},{24,32},{32,40},{40,48},{48,56},{56,64},{64,7... | collective-permute-start | bytes 1572872 | tf_op jit(solution)/shard_map/ppermute | solution.py:12
  115.2 2.2 %copy-start.2 = (f32[2048,512]{1,0:T(8,128)S(1)}, f32[2048,512]{1,0:T(8,128)}, u32[]{:S(2)}) copy-start(f32[2048,512]{1,0:T(8,128)} %get-tuple-element.15) | copy-start | bytes 12582916
  127.4 2.2 %copy-start.1 = (f32[2048,512]{1,0:T(8,128)S(1)}, f32[2048,512]{1,0:T(8,128)}, u32[]{:S(2)}) copy-start(f32[2048,512]{1,0:T(8,128)} %copy-done) | copy-start | bytes 12582916
  129.6 3.2 %copy-start.5 = (f32[512,1024]{1,0:T(8,128)S(1)}, f32[512,1024]{1,0:T(8,128)}, u32[]{:S(2)}) copy-start(f32[512,1024]{1,0:T(8,128)} %get-tuple-element.19) | copy-start | bytes 6291460
  129.6 3.2 %copy-start.6 = (f32[512,1024]{1,0:T(8,128)S(1)}, f32[512,1024]{1,0:T(8,128)}, u32[]{:S(2)}) copy-start(f32[512,1024]{1,0:T(8,128)} %get-tuple-element.20) | copy-start | bytes 6291460
  129.6 4.4 %copy-start.7 = (f32[1024,512]{1,0:T(8,128)S(1)}, f32[1024,512]{1,0:T(8,128)}, u32[]{:S(2)}) copy-start(f32[1024,512]{1,0:T(8,128)} %get-tuple-element.13) | copy-start | bytes 6291460
  129.6 5.0 %copy-start.8 = (f32[1024,512]{1,0:T(8,128)S(1)}, f32[1024,512]{1,0:T(8,128)}, u32[]{:S(2)}) copy-start(f32[1024,512]{1,0:T(8,128)} %get-tuple-element.14) | copy-start | bytes 6291460
  129.6 5.6 %copy-start.9 = (f32[1024,512]{1,0:T(8,128)S(1)}, f32[1024,512]{1,0:T(8,128)}, u32[]{:S(2)}) copy-start(f32[1024,512]{1,0:T(8,128)} %get-tuple-element.12) | copy-start | bytes 6291460
  129.6 5.6 %copy-start.11 = (bf16[512,512]{1,0:T(8,128)(2,1)S(1)}, bf16[512,512]{1,0:T(8,128)(2,1)}, u32[]{:S(2)}) copy-start(bf16[512,512]{1,0:T(8,128)(2,1)} %param.6) | copy-start | bytes 1572868
Sparse Core Ops, SparseCore 0:
  147.7 54.5 reduce-scatter.1
where the time goes:
time: 212 us; the launch traced here: 209 us
  waiting for transfers between devices  96.4 us (45%)
  other arithmetic  39 us (18%)
  matrix products  32.1 us (15%)
  starting transfers between devices  18.8 us (9%)
  between operations  16.8 us (8%)
  local copies, waits for them, and re-layouts  6.11 us (3%)
    reduce_scatter x1, waiting for transfers between devices, on_device(): lax.psum_scatter(partial_sums.astype(jnp.bfloat16), 'ch', scatter_dimensi...  54.8 us
    ppermute x8, waiting for transfers between devices, passed_along(): lax.ppermute(value, axis, [(source, source + steps) for source in range(i...  41.7 us
    ppermute x8, starting transfers between devices, passed_along(): lax.ppermute(value, axis, [(source, source + steps) for source in range(i...  18.8 us
    sub x5, other arithmetic, complex_product(): real_in * real_kern - imag_in * imag_kern  18.3 us
    dot_general x4, matrix products, segment_kernels(): jnp.dot(forward, filters[offset * block_len:(offset + 1) * block_len], pr...  11.4 us
    cos x1, other arithmetic, tables(): jnp.cos(angles_back)  10.6 us
    another operation x1, other arithmetic  8.54 us
    dot_general x1, matrix products, on_device(): jnp.dot(gated_rows, out_weight, preferred_element_type=jnp.float32)  6.49 us
  transfers between devices with their start and end apart: 9, of which 7 were waited for; matrix products, arithmetic and copies ran while one was open for 25% of the time, Pallas kernels for 0%

commit v1 on v0

v1 whole, which is shorter than its diff:
```python
import functools
import math

import jax
import jax.numpy as jnp
import ml_dtypes
import numpy as np
from jax import lax
from jax.experimental import pallas as pl
from jax.experimental.pallas import tpu as pltpu
from jax.sharding import PartitionSpec as P

MESH = pl.DeviceIdType.MESH
BF16, F32 = jnp.bfloat16, jnp.float32

BLK = 512
HALF = 256
NC = BLK // HALF
TAG = 16
ROWS = BLK + TAG
HC = 4
GC = 2
GR = BLK // GC
REACH = 4


def tables():
    period = 2 * BLK
    order = np.concatenate([np.arange(0, BLK, 2), np.arange(1, BLK, 2)])

    def angle(freq, pos):
        return (np.float32(2.0 * math.pi / period) * ((freq * pos) % period).astype(np.float32)).astype(np.float32)

    forward_angles = angle(order[:, None], np.arange(BLK)[None, :])
    real, imag = np.cos(forward_angles), -np.sin(forward_angles)
    imag[0] = np.cos(angle(np.full((1, 1), BLK), np.arange(BLK)[None, :]))[0]
    forward = np.concatenate([real, imag], 0).astype(ml_dtypes.bfloat16)
    out_rows = np.arange(BLK)[:, None] + BLK
    back_angles = angle(out_rows, order[None, :])
    real, imag = 2 * np.cos(back_angles), -2 * np.sin(back_angles)
    real[:, 0] = 1.0
    imag[:, 0] = np.cos(angle(out_rows, np.full((1, 1), BLK)))[:, 0]
    backward = (np.concatenate([real, imag], 1) / np.float32(period)).astype(ml_dtypes.bfloat16)
    return forward, backward


def kernel(seg_ref, q_hbm, k_hbm, v_hbm, filt_hbm, w_hbm, fwd_hbm, bwd_hbm, out_ref,
           q, k, v, filt, fwd, bwd, halo, kern, spec, acc, gated, wts, part, ysend, yrecv, lsem, ssem, rsem):
    ctx, ch = lax.axis_index("ctx"), lax.axis_index("ch")
    z, yh, core = ctx // 4, (ctx // 2) % 2, ctx % 2
    yl, x = ch // 4, ch % 4
    sibling = (z * 4 + yh * 2 + 1 - core, ch)
    y_pair = (ctx, (1 - yl) * 4 + x)
    y_far = (z * 4 + (1 - yh) * 2 + core, ch)
    z_next, z_prev = (((z + 1) % 8) * 4 + yh * 2 + core, ch), (((z + 7) % 8) * 4 + yh * 2 + core, ch)
    x_next, x_prev = (ctx, yl * 4 + (x + 1) % 4), (ctx, yl * 4 + (x + 3) % 4)
    x_far = (ctx, yl * 4 + (x + 2) % 4)

    barrier = pltpu.get_barrier_semaphore()
    for device in (sibling, y_pair, y_far, z_prev, x_next, x_prev, x_far):
        pl.semaphore_signal(barrier, inc=1, device_id=device, device_id_type=MESH)

    counter = [0]
    pending = []

    def number():
        counter[0] += 1
        return counter[0] - 1

    def remote(src, dst, sem, device):
        return pltpu.make_async_remote_copy(src_ref=src, dst_ref=dst, send_sem=ssem.at[sem], recv_sem=rsem.at[sem],
                                            device_id=device, device_id_type=MESH)

    def send(src, dst, device):
        copy = remote(src, dst, number(), device)
        copy.start()
        pending.append(copy)
        return copy

    local_count = [0]

    def load(src, dst):
        copy = pltpu.make_async_copy(src, dst, lsem.at[local_count[0]])
        local_count[0] += 1
        copy.start()
        return copy

    X, A, Y, B, Z = 0, 1, 2, 3, 4
    lanes = [pl.ds(c * HALF, HALF) for c in range(NC)]
    kv = [(load(k_hbm.at[:, lanes[c]], k.at[c]), load(v_hbm.at[:, lanes[c]], v.at[c])) for c in range(NC)]
    load_fwd = load(fwd_hbm, fwd)
    load_filt = [load(filt_hbm.at[:, lanes[c]], filt.at[c]) for c in range(NC)]
    load_bwd = load(bwd_hbm, bwd)
    load_q = [load(q_hbm.at[:, lanes[c]], q.at[c]) for c in range(NC)]

    def columns(r, xx):
        yy = yl if r == 0 else 1 - yl
        return pl.ds(pl.multiple_of((yy * 4 + xx) * BLK, BLK), BLK)

    load_w = [load(w_hbm.at[:, columns(r, x)], wts.at[0, :, pl.ds(r * BLK, BLK)]) for r in range(2)]

    tag = jnp.full((TAG, HALF), seg_ref[0].astype(F32)).astype(BF16)
    for c in range(NC):
        for copy in kv[c]:
            copy.wait()
        halo[X, c, pl.ds(0, BLK)] = (k[c].astype(F32) * v[c].astype(F32)).astype(BF16)
        halo[X, c, pl.ds(BLK, TAG)] = tag
    pl.semaphore_wait(barrier, 7)

    piece = BLK // HC
    pieces = [pl.ds(p * piece, piece + (TAG if p == HC - 1 else 0)) for p in range(HC)]
    z_copies, y_sems, s_sems = {}, {}, {}
    for c in range(NC):
        for p in range(HC):
            z_copies[c, p] = send(halo.at[X, c, pieces[p]], halo.at[Z, c, pieces[p]], z_next)
            y_sems[c, p] = number()
            own = remote(halo.at[X, c, pieces[p]], halo.at[Y, c, pieces[p]], y_sems[c, p], y_far)
            pending.append(own)

            @pl.when(yh == 0)
            def _():
                own.start()
        for slot in (A, B):
            s_sems[slot, c] = number()
        first = remote(halo.at[X, c], halo.at[A, c], s_sems[A, c], sibling)
        pending.append(first)

        @pl.when(core == 0)
        def _():
            first.start()

    half_rows = pl.ds(pl.multiple_of(core * HALF, HALF), HALF)
    w_copies = {}
    for slot, device, xx in ((1, x_next, (x + 1) % 4), (2, x_prev, (x + 3) % 4), (3, x_far, (x + 2) % 4)):
        for r in range(2):
            w_copies[slot, r] = send(w_hbm.at[half_rows, columns(r, xx)],
                                     wts.at[slot, half_rows, pl.ds(r * BLK, BLK)], device)

    def relay(c, p):
        @pl.when(yh == 1)
        def _():
            z_copies[c, p].wait_recv()
            remote(halo.at[Z, c, pieces[p]], halo.at[Y, c, pieces[p]], y_sems[c, p], y_far).start()

    def share(c):
        @pl.when(yh == 0)
        def _():
            for p in range(HC):
                z_copies[c, p].wait_recv()
        for p in range(HC):
            remote(halo.at[X, c, pieces[p]], halo.at[Y, c, pieces[p]], y_sems[c, p], y_far).wait_recv()

        @pl.when(core == 0)
        def _():
            remote(halo.at[Y, c], halo.at[B, c], s_sems[B, c], sibling).start()

        @pl.when(core == 1)
        def _():
            remote(halo.at[Y, c], halo.at[A, c], s_sems[A, c], sibling).start()
            remote(halo.at[Z, c], halo.at[B, c], s_sems[B, c], sibling).start()
        pending.append(remote(halo.at[Y, c], halo.at[B, c], s_sems[B, c], sibling))

    def quarter(g):
        return pl.ds(pl.multiple_of(g * HALF, HALF), HALF)

    def filter_kernels(c, d):
        taps = filt[c, pl.ds(d * BLK, BLK), :]

        @pl.loop(0, 4)
        def _(g):
            part_g = jnp.dot(fwd[quarter(g)], taps, preferred_element_type=F32)
            sign = (1 - 2 * (g % 2)).astype(F32)
            if d == 0:
                kern[0, c, quarter(g)] = sign * part_g
            else:
                kern[d, c, quarter(g)] += sign * part_g
            kern[d + 1, c, quarter(g)] = part_g

    def spectrum(c, d):
        block = halo[d, c, pl.ds(0, BLK)]
        if d:
            same = halo[d, c, pl.ds(BLK, TAG)].astype(F32)[0:1] == seg_ref[0].astype(F32)
            keep = jnp.where(jnp.logical_and(same, ctx >= d), 1.0, 0.0)

        @pl.loop(0, 4)
        def _(g):
            value = jnp.dot(fwd[quarter(g)], block, preferred_element_type=F32)
            spec[d, quarter(g)] = value * keep if d else value

    def product(c):
        def rows_at(start, rows, first):
            re_rows, im_rows = pl.ds(start, rows), pl.ds(start + BLK, rows)
            re, im = 0.0, 0.0
            if first:
                zeroth = lax.broadcasted_iota(jnp.int32, (rows, HALF), 0) == 0
            for d in range(REACH + 1):
                a_r, a_i = spec[d, re_rows], spec[d, im_rows]
                g_r, g_i = kern[d, c, re_rows], kern[d, c, im_rows]
                rr, ii, ri, ir = a_r * g_r, a_i * g_i, a_r * g_i, a_i * g_r
                if first:
                    re = re + (rr - jnp.where(zeroth, 0.0, ii))
                    im = im + jnp.where(zeroth, ii, ri + ir)
                else:
                    re = re + (rr - ii)
                    im = im + (ri + ir)
            acc[re_rows] = re.astype(BF16)
            acc[im_rows] = im.astype(BF16)

        rows_at(0, 16, True)

        @pl.loop(1, BLK // 16, unroll=1)
        def _(step):
            rows_at(pl.multiple_of(step * 16, 16), 16, False)

    g_copies = {}

    def gate(c, r):
        rows = pl.ds(r * GR, GR)
        value = jnp.dot(bwd[rows], acc[...], preferred_element_type=F32)
        gated[0, c, rows] = (q[c, rows].astype(F32) * value).astype(BF16)
        g_copies[1, c, r] = send(gated.at[0, c, rows], gated.at[1, c, rows], x_next)
        g_copies[2, c, r] = send(gated.at[0, c, rows], gated.at[2, c, rows], x_prev)

    def pass_on(c, r):
        low, high = pl.ds(r * GR, GR // 2), pl.ds(r * GR + GR // 2, GR // 2)
        g_copies[1, c, r].wait_recv()
        g_copies[3, c, r, 0] = send(gated.at[1, c, low], gated.at[3, c, low], x_next)
        g_copies[2, c, r].wait_recv()
        g_copies[3, c, r, 1] = send(gated.at[2, c, high], gated.at[3, c, high], x_prev)

    load_fwd.wait()
    load_filt[0].wait()
    for d in range(REACH):
        filter_kernels(0, d)
    spectrum(0, X)
    load_filt[1].wait()
    for p in range(HC):
        relay(0, p)
        filter_kernels(1, p)
    share(0)
    load_bwd.wait()
    load_q[0].wait()
    load_q[1].wait()

    for c in range(NC):
        spectrum(c, Y) if c == 0 else spectrum(c, X)
        if c == 0:
            relay(1, 0)
        else:
            spectrum(c, Y)
        spectrum(c, Z)
        if c == 0:
            relay(1, 1)
        for slot in (A, B):
            remote(halo.at[Y, c], halo.at[slot, c], s_sems[slot, c], sibling).wait_recv()
            spectrum(c, slot)
            if c == 0:
                relay(1, 2 if slot == A else 3)
        product(c)
        for r in range(GC):
            gate(c, r)
        if c == 0:
            share(1)

    for c in range(NC):
        for r in range(GC):
            pass_on(c, r)

    s_w = {}

    def weights_arrive(slot):
        for r in range(2):
            w_copies[slot, r].wait_recv()
        s_w[slot] = send(wts.at[slot, half_rows], wts.at[slot, half_rows], sibling)

    def project(slot, c, r, fresh):
        rows = pl.ds(r * GR, GR)

        @pl.loop(0, 4)
        def _(n):
            cols = quarter(n)
            value = jnp.dot(gated[slot, c, rows], wts[slot, pl.ds(c * HALF, HALF), cols], preferred_element_type=F32)
            if fresh:
                part[rows, cols] = value
            else:
                part[rows, cols] += value

    for copy in load_w:
        copy.wait()
    for c in range(NC):
        for r in range(GC):
            project(0, c, r, c == 0)
    for slot in (1, 2):
        weights_arrive(slot)
        s_w[slot].wait_recv()
        for c in range(NC):
            for r in range(GC):
                project(slot, c, r, False)
    weights_arrive(3)
    s_w[3].wait_recv()
    y_copies = []
    for r in range(GC):
        rows = pl.ds(r * GR, GR)
        for c in range(NC):
            for side in range(2):
                g_copies[3, c, r, side].wait_recv()
            project(3, c, r, False)
        ysend[rows] = part[rows, pl.ds(BLK, BLK)].astype(BF16)
        y_copies.append(send(ysend.at[rows], yrecv.at[rows], y_pair))
    for r in range(GC):
        rows = pl.ds(r * GR, GR)
        y_copies[r].wait_recv()
        out_ref[rows] = (part[rows, pl.ds(0, BLK)] + yrecv[rows].astype(F32)).astype(BF16)
    for copy in pending:
        copy.wait_send()


def on_device(query, keys, values, filters, segment_ids, out_weight):
    forward, backward = tables()
    anywhere = pl.BlockSpec(memory_space=pl.ANY)
    return pl.pallas_call(
        kernel,
        out_shape=jax.ShapeDtypeStruct((BLK, BLK), BF16),
        in_specs=[pl.BlockSpec(memory_space=pltpu.SMEM)] + [anywhere] * 7,
        out_specs=pl.BlockSpec(memory_space=pltpu.VMEM),
        scratch_shapes=[
            pltpu.VMEM((NC, BLK, HALF), BF16),
            pltpu.VMEM((NC, BLK, HALF), BF16),
            pltpu.VMEM((NC, BLK, HALF), BF16),
            pltpu.VMEM((NC, REACH * BLK, HALF), BF16),
            pltpu.VMEM((2 * BLK, BLK), BF16),
            pltpu.VMEM((BLK, 2 * BLK), BF16),
            pltpu.VMEM((REACH + 1, NC, ROWS, HALF), BF16),
            pltpu.VMEM((REACH + 1, NC, 2 * BLK, HALF), F32),
            pltpu.VMEM((REACH + 1, 2 * BLK, HALF), F32),
            pltpu.VMEM((2 * BLK, HALF), BF16),
            pltpu.VMEM((4, NC, BLK, HALF), BF16),
            pltpu.VMEM((4, BLK, 2 * BLK), BF16),
            pltpu.VMEM((BLK, 2 * BLK), F32),
            pltpu.VMEM((BLK, BLK), BF16),
            pltpu.VMEM((BLK, BLK), BF16),
            pltpu.SemaphoreType.DMA((16,)),
            pltpu.SemaphoreType.DMA((64,)),
            pltpu.SemaphoreType.DMA((64,)),
        ],
        compiler_params=pltpu.CompilerParams(collective_id=0, has_side_effects=True, vmem_limit_bytes=56 * 2**20),
        name="hyena",
    )(segment_ids, query, keys, values, filters, out_weight, jnp.asarray(forward), jnp.asarray(backward))


def solution(mesh):
    in_specs = (
        P("ctx", "ch"),
        P("ctx", "ch"),
        P("ctx", "ch"),
        P(None, "ch"),
        P("ctx"),
        P("ch", None),
    )
    return jax.shard_map(on_device, mesh=mesh, in_specs=in_specs, out_specs=P("ctx", "ch"), check_vma=False)
```

time: 212 us -> 76.3 us (0.36)
  the two profiles are of different devices: /device:TPU:128 before, /device:TPU:1 now
where the time goes in v1:
time: 76.3 us; the launch traced here: 76.1 us
  Pallas kernels  73.6 us (96%)
  local copies, waits for them, and re-layouts  1.87 us (2%)
    pallas_call x1, Pallas kernels, on_device(): pl.pallas_call(kernel, out_shape=jax.ShapeDtypeStruct((BLK, BLK), BF16),...  73.6 us
    unnamed x1, local copies, waits for them, and re-layouts  1.87 us

profile of v1, /device:TPU:1, one launch (start us, length us, event | category | flops | bytes accessed | tf_op | source)
XLA Modules:
  0.0 76.1 jit_solution(6448732020203838638)
XLA Ops:
  0.7 73.6 %hyena.1 = bf16[512,512]{1,0:T(8,128)(2,1)} custom-call(s32[1]{0:T(128)S(6)} %copy.10.seg_ref, bf16[512,512]{1,0:T(8,128)(2,1)} %q_hbm.1, bf16[512,512]{1,0:T(8,128)(2,1)} %k_hbm.1, bf16[512,512]{1,0:T(8,128)(2,1)} %v_hbm.1, bf16[2048,512]{1,0:T(8,128)(2,1)} %filt_hbm.1, bf16[512,4096]{1,0:T(8,128)(2,1)} %w_hbm.1, bf16[1024,512]{1,0:T(8,128)(2,1)} %constant.4.clone.fwd_hbm, ...), custom_call_target="tpu_custom_call" | custom-call | tf_op jit(solution)/shard_map/hyena/pallas_call | solution.py:321
  74.3 1.9 %copy.11 = bf16[512,512]{1,0:T(8,128)(2,1)} copy(bf16[512,512]{1,0:T(8,128)(2,1)} %hyena.1) | data formatting | bytes 1048576

commit v2 on v1

v2 whole, which is shorter than its diff:
```python
import functools
import math

import jax
import jax.numpy as jnp
import ml_dtypes
import numpy as np
from jax import lax
from jax.experimental import pallas as pl
from jax.experimental.pallas import tpu as pltpu
from jax.sharding import PartitionSpec as P

MESH = pl.DeviceIdType.MESH
BF16, F32 = jnp.bfloat16, jnp.float32

BLK = 512
HALF = 256
NC = BLK // HALF
TAG = 16
ROWS = BLK + TAG
HC = 4
GC = 4
GR = BLK // GC
QUARTER = BLK // 4
REACH = 4


def tables():
    period = 2 * BLK
    order = np.concatenate([np.arange(0, BLK, 2), np.arange(1, BLK, 2)])

    def angle(freq, pos):
        return (np.float32(2.0 * math.pi / period) * ((freq * pos) % period).astype(np.float32)).astype(np.float32)

    forward_angles = angle(order[:, None], np.arange(BLK)[None, :])
    real, imag = np.cos(forward_angles), -np.sin(forward_angles)
    imag[0] = np.cos(angle(np.full((1, 1), BLK), np.arange(BLK)[None, :]))[0]
    forward = np.concatenate([real, imag], 0).astype(ml_dtypes.bfloat16)
    out_rows = np.arange(BLK)[:, None] + BLK
    back_angles = angle(out_rows, order[None, :])
    real, imag = 2 * np.cos(back_angles), -2 * np.sin(back_angles)
    real[:, 0] = 1.0
    imag[:, 0] = np.cos(angle(out_rows, np.full((1, 1), BLK)))[:, 0]
    backward = (np.concatenate([real, imag], 1) / np.float32(period)).astype(ml_dtypes.bfloat16)
    return forward, backward


def kernel(seg_ref, q_hbm, k_hbm, v_hbm, filt_hbm, w_hbm, fwd_hbm, bwd_hbm, out_ref,
           q, k, v, filt, fwd, bwd, halo, kern, spec, acc, gated, wts, part, ysend, yrecv, lsem, ssem, rsem):
    ctx, ch = lax.axis_index("ctx"), lax.axis_index("ch")
    z, yh, core = ctx // 4, (ctx // 2) % 2, ctx % 2
    yl, x = ch // 4, ch % 4
    zpar = z % 2
    sibling = (z * 4 + yh * 2 + 1 - core, ch)
    y_pair = (ctx, (1 - yl) * 4 + x)
    y_far = (z * 4 + (1 - yh) * 2 + core, ch)
    z_next, z_prev = (((z + 1) % 8) * 4 + yh * 2 + core, ch), (((z + 7) % 8) * 4 + yh * 2 + core, ch)
    z_pair = ((z + 1 - 2 * zpar) * 4 + yh * 2 + core, ch)
    x_next, x_prev = (ctx, yl * 4 + (x + 1) % 4), (ctx, yl * 4 + (x + 3) % 4)
    x_far = (ctx, yl * 4 + (x + 2) % 4)
    first_z, last_z = z == 0, z == 7

    def signal(device):
        pl.semaphore_signal(barrier, inc=1, device_id=device, device_id_type=MESH)

    barrier = pltpu.get_barrier_semaphore()
    for device in (sibling, y_pair, y_far, x_next, x_prev, x_far):
        signal(device)

    @pl.when(jnp.logical_not(first_z))
    def _():
        signal(z_prev)

    @pl.when(jnp.logical_not(last_z))
    def _():
        signal(z_next)

    counter = [0, 0]
    always, by_condition = [], []

    def number():
        counter[0] += 1
        return counter[0] - 1

    def remote(src, dst, sem, device):
        return pltpu.make_async_remote_copy(src_ref=src, dst_ref=dst, send_sem=ssem.at[sem], recv_sem=rsem.at[sem],
                                            device_id=device, device_id_type=MESH)

    def send(src, dst, device):
        copy = remote(src, dst, number(), device)
        copy.start()
        always.append(copy)
        return copy

    def load(src, dst):
        copy = pltpu.make_async_copy(src, dst, lsem.at[counter[1]])
        counter[1] += 1
        copy.start()
        return copy

    X, A, Y, B, Z = 0, 1, 2, 3, 4
    lanes = [pl.ds(c * HALF, HALF) for c in range(NC)]
    kv = [(load(k_hbm.at[:, lanes[c]], k.at[c]), load(v_hbm.at[:, lanes[c]], v.at[c])) for c in range(NC)]
    load_fwd = load(fwd_hbm, fwd)
    load_filt = [load(filt_hbm.at[:, lanes[c]], filt.at[c]) for c in range(NC)]
    load_bwd = load(bwd_hbm, bwd)
    load_q = [load(q_hbm.at[:, lanes[c]], q.at[c]) for c in range(NC)]

    def columns(r, xx):
        yy = yl if r == 0 else 1 - yl
        return pl.ds(pl.multiple_of((yy * 4 + xx) * BLK, BLK), BLK)

    load_w = [load(w_hbm.at[pl.ds(c * HALF, HALF), columns(r, x)], wts.at[c, pl.ds(0, HALF), pl.ds(r * BLK, BLK)])
              for c in range(NC) for r in range(2)]

    @pl.when(first_z)
    def _():
        halo[Z] = jnp.zeros((NC, ROWS, HALF), BF16)

        @pl.when(yh == 0)
        def _():
            halo[Y] = jnp.zeros((NC, ROWS, HALF), BF16)

    tag = jnp.full((TAG, HALF), seg_ref[0].astype(F32)).astype(BF16)
    for c in range(NC):
        for copy in kv[c]:
            copy.wait()
        halo[X, c, pl.ds(0, BLK)] = (k[c].astype(F32) * v[c].astype(F32)).astype(BF16)
        halo[X, c, pl.ds(BLK, TAG)] = tag
    pl.semaphore_wait(barrier, 8 - first_z.astype(jnp.int32) - last_z.astype(jnp.int32))

    piece = BLK // HC
    pieces = [pl.ds(p * piece, piece + (TAG if p == HC - 1 else 0)) for p in range(HC)]
    z_copies, y_copies, s_copies, s_sems = {}, {}, {}, {}
    gets_y = jnp.logical_or(yh == 1, jnp.logical_not(first_z))
    gives_y = jnp.logical_or(yh == 0, jnp.logical_not(first_z))
    for c in range(NC):
        for p, rows in enumerate(pieces):
            z_copies[c, p] = remote(halo.at[X, c, rows], halo.at[Z, c, rows], number(), z_next)
            y_copies[c, p] = [remote(halo.at[src, c, rows], halo.at[Y, c, rows], counter[0], y_far) for src in (X, Z)]
            number()
            s_sems[A, c, p], s_sems[B, c, p] = number(), number()
            by_condition.append((jnp.logical_not(last_z), z_copies[c, p]))
            by_condition.append((gives_y, y_copies[c, p][0]))
            for slot in (A, B):
                s_copies[slot, c, p] = remote(halo.at[X, c, rows], halo.at[slot, c, rows], s_sems[slot, c, p], sibling)
                always.append(s_copies[slot, c, p])

            @pl.when(jnp.logical_not(last_z))
            def _():
                z_copies[c, p].start()

            @pl.when(yh == 0)
            def _():
                y_copies[c, p][0].start()

            @pl.when(core == 0)
            def _():
                s_copies[A, c, p].start()

    w_copies, w_z, w_sib = {}, {}, {}

    def w_rows(slot, parity):
        return pl.ds(pl.multiple_of(slot * HALF + parity * QUARTER, QUARTER), QUARTER)

    own_rows = pl.ds(pl.multiple_of(core * HALF + zpar * QUARTER, QUARTER), QUARTER)
    for slot, device, xx in ((1, x_next, (x + 1) % 4), (2, x_prev, (x + 3) % 4), (3, x_far, (x + 2) % 4)):
        for r in range(2):
            w_copies[slot, r] = send(w_hbm.at[own_rows, columns(r, xx)],
                                     wts.at[core, w_rows(slot, zpar), pl.ds(r * BLK, BLK)], device)

    def weights_on(slot):
        for r in range(2):
            w_copies[slot, r].wait_recv()
        mine = wts.at[core, w_rows(slot, zpar)]
        w_z[slot] = send(mine, mine, z_pair)
        w_sib[slot, 0] = send(mine, mine, sibling)

    def weights_share(slot):
        w_z[slot].wait_recv()
        theirs = wts.at[core, w_rows(slot, 1 - zpar)]
        w_sib[slot, 1] = send(theirs, theirs, sibling)

    def weights_wait(slot):
        for part_of in range(2):
            w_sib[slot, part_of].wait_recv()

    def z_arrives(c, p):
        rows = pieces[p]

        @pl.when(jnp.logical_not(first_z))
        def _():
            z_copies[c, p].wait_recv()

            @pl.when(yh == 1)
            def _():
                y_copies[c, p][1].start()

        @pl.when(core == 1)
        def _():
            remote(halo.at[Z, c, rows], halo.at[B, c, rows], s_sems[B, c, p], sibling).start()

    def y_arrives(c, p):
        rows = pieces[p]

        @pl.when(gets_y)
        def _():
            y_copies[c, p][0].wait_recv()

        @pl.when(core == 0)
        def _():
            remote(halo.at[Y, c, rows], halo.at[B, c, rows], s_sems[B, c, p], sibling).start()

        @pl.when(core == 1)
        def _():
            remote(halo.at[Y, c, rows], halo.at[A, c, rows], s_sems[A, c, p], sibling).start()

    def shared(c, slot):
        for p in range(HC):
            s_copies[slot, c, p].wait_recv()

    even_odd = [pl.ds(g * HALF, HALF) for g in range(4)]

    def filter_kernels(c, d):
        taps = filt[c, pl.ds(d * BLK, BLK), :]
        for g, rows in enumerate(even_odd):
            part_g = jnp.dot(fwd[rows], taps, preferred_element_type=F32)
            turned = -part_g if g % 2 else part_g
            kern[d, c, rows] = kern[d, c, rows] + turned if d else turned
            kern[d + 1, c, rows] = part_g

    def spectrum(c, d):
        block = halo[d, c, pl.ds(0, BLK)]
        if d:
            same = halo[d, c, pl.ds(BLK, TAG)].astype(F32)[0:1] == seg_ref[0].astype(F32)
            keep = jnp.where(jnp.logical_and(same, ctx >= d), 1.0, 0.0)
        for rows in even_odd:
            value = jnp.dot(fwd[rows], block, preferred_element_type=F32)
            spec[d, rows] = value * keep if d else value

    def product(c):
        def rows_at(start, rows, first):
            re_rows, im_rows = pl.ds(start, rows), pl.ds(start + BLK, rows)
            re, im = 0.0, 0.0
            if first:
                zeroth = lax.broadcasted_iota(jnp.int32, (rows, HALF), 0) == 0
            for d in range(REACH + 1):
                a_r, a_i = spec[d, re_rows], spec[d, im_rows]
                g_r, g_i = kern[d, c, re_rows], kern[d, c, im_rows]
                rr, ii, ri, ir = a_r * g_r, a_i * g_i, a_r * g_i, a_i * g_r
                if first:
                    re = re + (rr - jnp.where(zeroth, 0.0, ii))
                    im = im + jnp.where(zeroth, ii, ri + ir)
                else:
                    re = re + (rr - ii)
                    im = im + (ri + ir)
            acc[re_rows] = re.astype(BF16)
            acc[im_rows] = im.astype(BF16)

        @pl.loop(0, BLK // 64)
        def _(step):
            for u in range(4):
                rows_at(pl.multiple_of(step * 64 + u * 16, 16), 16, False)

        rows_at(0, 16, True)

    g_copies = {}

    def slot_lanes(slot):
        return pl.ds(slot * HALF, HALF)

    def gate(c, r):
        rows = pl.ds(r * GR, GR)
        value = jnp.dot(bwd[rows], acc[...], preferred_element_type=F32)
        gated[c, rows, slot_lanes(0)] = (q[c, rows].astype(F32) * value).astype(BF16)
        own = gated.at[c, rows, slot_lanes(0)]
        g_copies[1, c, r] = send(own, gated.at[c, rows, slot_lanes(1)], x_next)
        g_copies[2, c, r] = send(own, gated.at[c, rows, slot_lanes(2)], x_prev)

    def pass_on(c, r):
        low, high = pl.ds(r * GR, GR // 2), pl.ds(r * GR + GR // 2, GR // 2)
        for slot, rows, device in ((1, low, x_next), (2, high, x_prev)):
            g_copies[slot, c, r].wait_recv()
            g_copies[3, c, r, slot] = send(gated.at[c, rows, slot_lanes(slot)], gated.at[c, rows, slot_lanes(3)], device)

    def gathered(c, r):
        for slot in (1, 2):
            g_copies[3, c, r, slot].wait_recv()

    load_fwd.wait()
    load_filt[0].wait()
    spectrum(0, X)
    for d in range(REACH):
        filter_kernels(0, d)
    load_filt[1].wait()
    for p in range(HC):
        z_arrives(0, p)
        filter_kernels(1, p)
    load_bwd.wait()
    load_q[0].wait()
    load_q[1].wait()
    for p in range(HC):
        y_arrives(0, p)
    spectrum(0, Z)
    z_arrives(1, 0)
    spectrum(0, Y)
    z_arrives(1, 1)
    shared(0, A)
    spectrum(0, A)
    z_arrives(1, 2)
    shared(0, B)
    spectrum(0, B)
    z_arrives(1, 3)
    product(0)
    for r in range(GC):
        gate(0, r)
    weights_on(1)
    weights_on(2)
    spectrum(1, X)
    for p in range(HC):
        y_arrives(1, p)
    spectrum(1, Z)
    spectrum(1, Y)
    shared(1, A)
    spectrum(1, A)
    shared(1, B)
    spectrum(1, B)
    product(1)
    for r in range(GC):
        gate(1, r)
    weights_on(3)

    own_cols, other_cols = pl.ds(0, BLK), pl.ds(BLK, BLK)

    def project(c, rows, cols):
        return jnp.dot(gated[c, rows], wts[c, :, cols], preferred_element_type=F32)

    for r in range(GC):
        pass_on(0, r)
    for copy in load_w:
        copy.wait()
    for slot in (1, 2, 3):
        weights_share(slot)
    for r in range(GC):
        pass_on(1, r)
    for slot in (1, 2, 3):
        weights_wait(slot)
    for r in range(GC):
        gathered(0, r)
    everything = pl.ds(0, BLK)
    for cols in (other_cols, own_cols):
        part[:, cols] = project(0, everything, cols)
    swaps = []
    for r in range(GC):
        rows = pl.ds(r * GR, GR)
        gathered(1, r)
        ysend[rows] = (part[rows, other_cols] + project(1, rows, other_cols)).astype(BF16)
        swaps.append(send(ysend.at[rows], yrecv.at[rows], y_pair))
    part[:, own_cols] += project(1, everything, own_cols)
    for r in range(GC):
        rows = pl.ds(r * GR, GR)
        swaps[r].wait_recv()
        out_ref[rows] = (part[rows, own_cols] + yrecv[rows].astype(F32)).astype(BF16)
    for copy in always:
        copy.wait_send()
    for condition, copy in by_condition:
        @pl.when(condition)
        def _():
            copy.wait_send()


def on_device(query, keys, values, filters, segment_ids, out_weight):
    forward, backward = tables()
    anywhere = pl.BlockSpec(memory_space=pl.ANY)
    return pl.pallas_call(
        kernel,
        out_shape=jax.ShapeDtypeStruct((BLK, BLK), BF16),
        in_specs=[pl.BlockSpec(memory_space=pltpu.SMEM)] + [anywhere] * 7,
        out_specs=pl.BlockSpec(memory_space=pltpu.VMEM),
        scratch_shapes=[
            pltpu.VMEM((NC, BLK, HALF), BF16),
            pltpu.VMEM((NC, BLK, HALF), BF16),
            pltpu.VMEM((NC, BLK, HALF), BF16),
            pltpu.VMEM((NC, REACH * BLK, HALF), BF16),
            pltpu.VMEM((2 * BLK, BLK), BF16),
            pltpu.VMEM((BLK, 2 * BLK), BF16),
            pltpu.VMEM((REACH + 1, NC, ROWS, HALF), BF16),
            pltpu.VMEM((REACH + 1, NC, 2 * BLK, HALF), F32),
            pltpu.VMEM((REACH + 1, 2 * BLK, HALF), F32),
            pltpu.VMEM((2 * BLK, HALF), BF16),
            pltpu.VMEM((NC, BLK, 4 * HALF), BF16),
            pltpu.VMEM((NC, 4 * HALF, 2 * BLK), BF16),
            pltpu.VMEM((BLK, 2 * BLK), F32),
            pltpu.VMEM((BLK, BLK), BF16),
            pltpu.VMEM((BLK, BLK), BF16),
            pltpu.SemaphoreType.DMA((16,)),
            pltpu.SemaphoreType.DMA((96,)),
            pltpu.SemaphoreType.DMA((96,)),
        ],
        compiler_params=pltpu.CompilerParams(collective_id=0, has_side_effects=True, vmem_limit_bytes=56 * 2**20),
        name="hyena",
    )(segment_ids, query, keys, values, filters, out_weight, jnp.asarray(forward), jnp.asarray(backward))


def solution(mesh):
    in_specs = (
        P("ctx", "ch"),
        P("ctx", "ch"),
        P("ctx", "ch"),
        P(None, "ch"),
        P("ctx"),
        P("ch", None),
    )
    return jax.shard_map(on_device, mesh=mesh, in_specs=in_specs, out_specs=P("ctx", "ch"), check_vma=False)
```

time: 76.3 us -> 61.4 us (0.80)
  the two profiles are of different devices: /device:TPU:1 before, /device:TPU:128 now
where the time goes in v2:
time: 61.4 us; the launch traced here: 61.2 us
  Pallas kernels  58.7 us (96%)
  local copies, waits for them, and re-layouts  1.87 us (3%)
  between operations  0.66 us (1%)
    pallas_call x1, Pallas kernels, on_device(): pl.pallas_call(kernel, out_shape=jax.ShapeDtypeStruct((BLK, BLK), BF16),...  58.7 us
    unnamed x1, local copies, waits for them, and re-layouts  1.87 us

profile of v2, /device:TPU:128, one launch (start us, length us, event | category | flops | bytes accessed | tf_op | source)
XLA Modules:
  0.0 61.2 jit_solution(15750614873976928288)
XLA Ops:
  0.7 58.7 %hyena.1 = bf16[512,512]{1,0:T(8,128)(2,1)} custom-call(s32[1]{0:T(128)S(6)} %copy.10.seg_ref, bf16[512,512]{1,0:T(8,128)(2,1)} %q_hbm.1, bf16[512,512]{1,0:T(8,128)(2,1)} %k_hbm.1, bf16[512,512]{1,0:T(8,128)(2,1)} %v_hbm.1, bf16[2048,512]{1,0:T(8,128)(2,1)} %filt_hbm.1, bf16[512,4096]{1,0:T(8,128)(2,1)} %w_hbm.1, bf16[1024,512]{1,0:T(8,128)(2,1)} %constant.4.clone.fwd_hbm, ...), custom_call_target="tpu_custom_call" | custom-call | tf_op jit(solution)/shard_map/hyena/pallas_call | solution.py:375
  59.4 1.9 %copy.11 = bf16[512,512]{1,0:T(8,128)(2,1)} copy(bf16[512,512]{1,0:T(8,128)(2,1)} %hyena.1) | data formatting | bytes 1048576

commit v3 on v2

--- a/solution.py
+++ b/solution.py
@@ -164,26 +164,28 @@
         return pl.ds(pl.multiple_of(slot * HALF + parity * QUARTER, QUARTER), QUARTER)
 
     own_rows = pl.ds(pl.multiple_of(core * HALF + zpar * QUARTER, QUARTER), QUARTER)
-    for slot, device, xx in ((1, x_next, (x + 1) % 4), (2, x_prev, (x + 3) % 4), (3, x_far, (x + 2) % 4)):
-        for r in range(2):
+    for r in (1, 0):
+        for slot, device, xx in ((1, x_next, (x + 1) % 4), (2, x_prev, (x + 3) % 4), (3, x_far, (x + 2) % 4)):
             w_copies[slot, r] = send(w_hbm.at[own_rows, columns(r, xx)],
                                      wts.at[core, w_rows(slot, zpar), pl.ds(r * BLK, BLK)], device)
 
-    def weights_on(slot):
-        for r in range(2):
+    def weights_on(r):
+        for slot in (1, 2, 3):
             w_copies[slot, r].wait_recv()
-        mine = wts.at[core, w_rows(slot, zpar)]
-        w_z[slot] = send(mine, mine, z_pair)
-        w_sib[slot, 0] = send(mine, mine, sibling)
-
-    def weights_share(slot):
-        w_z[slot].wait_recv()
-        theirs = wts.at[core, w_rows(slot, 1 - zpar)]
-        w_sib[slot, 1] = send(theirs, theirs, sibling)
-
-    def weights_wait(slot):
-        for part_of in range(2):
-            w_sib[slot, part_of].wait_recv()
+            mine = wts.at[core, w_rows(slot, zpar), pl.ds(r * BLK, BLK)]
+            w_z[slot, r] = send(mine, mine, z_pair)
+            w_sib[slot, r, 0] = send(mine, mine, sibling)
+
+    def weights_share(r):
+        for slot in (1, 2, 3):
+            w_z[slot, r].wait_recv()
+            theirs = wts.at[core, w_rows(slot, 1 - zpar), pl.ds(r * BLK, BLK)]
+            w_sib[slot, r, 1] = send(theirs, theirs, sibling)
+
+    def weights_wait(r):
+        for slot in (1, 2, 3):
+            for part_of in range(2):
+                w_sib[slot, r, part_of].wait_recv()
 
     def z_arrives(c, p):
         rows = pieces[p]
@@ -273,6 +275,9 @@
         rows = pl.ds(r * GR, GR)
         value = jnp.dot(bwd[rows], acc[...], preferred_element_type=F32)
         gated[c, rows, slot_lanes(0)] = (q[c, rows].astype(F32) * value).astype(BF16)
+
+    def give(c, r):
+        rows = pl.ds(r * GR, GR)
         own = gated.at[c, rows, slot_lanes(0)]
         g_copies[1, c, r] = send(own, gated.at[c, rows, slot_lanes(1)], x_next)
         g_copies[2, c, r] = send(own, gated.at[c, rows, slot_lanes(2)], x_prev)
@@ -299,6 +304,7 @@
     load_bwd.wait()
     load_q[0].wait()
     load_q[1].wait()
+    weights_on(1)
     for p in range(HC):
         y_arrives(0, p)
     spectrum(0, Z)
@@ -314,49 +320,63 @@
     product(0)
     for r in range(GC):
         gate(0, r)
-    weights_on(1)
-    weights_on(2)
+        give(0, r)
     spectrum(1, X)
+    spectrum(1, Z)
+    weights_on(0)
     for p in range(HC):
         y_arrives(1, p)
-    spectrum(1, Z)
+    pass_on(0, 0)
+    pass_on(0, 1)
     spectrum(1, Y)
     shared(1, A)
     spectrum(1, A)
     shared(1, B)
     spectrum(1, B)
     product(1)
-    for r in range(GC):
-        gate(1, r)
-    weights_on(3)
+    gate(1, 0)
+    give(1, 0)
+    pass_on(0, 2)
+    gate(1, 1)
+    give(1, 1)
+    pass_on(0, 3)
+    gate(1, 2)
+    gate(1, 3)
 
     own_cols, other_cols = pl.ds(0, BLK), pl.ds(BLK, BLK)
 
     def project(c, rows, cols):
         return jnp.dot(gated[c, rows], wts[c, :, cols], preferred_element_type=F32)
 
-    for r in range(GC):
-        pass_on(0, r)
-    for copy in load_w:
-        copy.wait()
-    for slot in (1, 2, 3):
-        weights_share(slot)
-    for r in range(GC):
-        pass_on(1, r)
-    for slot in (1, 2, 3):
-        weights_wait(slot)
-    for r in range(GC):
-        gathered(0, r)
     everything = pl.ds(0, BLK)
-    for cols in (other_cols, own_cols):
-        part[:, cols] = project(0, everything, cols)
     swaps = []
-    for r in range(GC):
+
+    def swap(r):
         rows = pl.ds(r * GR, GR)
         gathered(1, r)
         ysend[rows] = (part[rows, other_cols] + project(1, rows, other_cols)).astype(BF16)
         swaps.append(send(ysend.at[rows], yrecv.at[rows], y_pair))
-    part[:, own_cols] += project(1, everything, own_cols)
+
+    weights_share(1)
+    for copy in load_w:
+        copy.wait()
+    pass_on(1, 0)
+    give(1, 2)
+    pass_on(1, 1)
+    give(1, 3)
+    for r in range(GC):
+        gathered(0, r)
+    weights_wait(1)
+    part[:, other_cols] = project(0, everything, other_cols)
+    swap(0)
+    pass_on(1, 2)
+    swap(1)
+    pass_on(1, 3)
+    swap(2)
+    swap(3)
+    weights_share(0)
+    weights_wait(0)
+    part[:, own_cols] = project(0, everything, own_cols) + project(1, everything, own_cols)
     for r in range(GC):
         rows = pl.ds(r * GR, GR)
         swaps[r].wait_recv()

time: 61.4 us -> 53.3 us (0.87)
  Pallas kernels: 58.7 us -> 50.7 us
    pallas_call x1, Pallas kernels: 58.7 us -> 50.7 us  [on_device(): pl.pallas_call(kernel, out_shape=jax.ShapeDtypeStruct((BLK, BLK), BF16),...]
where the time goes in v3:
time: 53.3 us; the launch traced here: 53.2 us
  Pallas kernels  50.7 us (95%)
  local copies, waits for them, and re-layouts  1.87 us (4%)
  between operations  0.66 us (1%)
    pallas_call x1, Pallas kernels, on_device(): pl.pallas_call(kernel, out_shape=jax.ShapeDtypeStruct((BLK, BLK), BF16),...  50.7 us
    unnamed x1, local copies, waits for them, and re-layouts  1.87 us

profile of v3, /device:TPU:128, one launch (start us, length us, event | category | flops | bytes accessed | tf_op | source)
XLA Modules:
  0.0 53.2 jit_solution(8009259747982789506)
XLA Ops:
  0.7 50.7 %hyena.1 = bf16[512,512]{1,0:T(8,128)(2,1)} custom-call(s32[1]{0:T(128)S(6)} %copy.10.seg_ref, bf16[512,512]{1,0:T(8,128)(2,1)} %q_hbm.1, bf16[512,512]{1,0:T(8,128)(2,1)} %k_hbm.1, bf16[512,512]{1,0:T(8,128)(2,1)} %v_hbm.1, bf16[2048,512]{1,0:T(8,128)(2,1)} %filt_hbm.1, bf16[512,4096]{1,0:T(8,128)(2,1)} %w_hbm.1, bf16[1024,512]{1,0:T(8,128)(2,1)} %constant.4.clone.fwd_hbm, ...), custom_call_target="tpu_custom_call" | custom-call | tf_op jit(solution)/shard_map/hyena/pallas_call | solution.py:395
  51.4 1.9 %copy.11 = bf16[512,512]{1,0:T(8,128)(2,1)} copy(bf16[512,512]{1,0:T(8,128)(2,1)} %hyena.1) | data formatting | bytes 1048576

commit v4 on v3

--- a/solution.py
+++ b/solution.py
@@ -18,7 +18,8 @@
 NC = BLK // HALF
 TAG = 16
 ROWS = BLK + TAG
-HC = 4
+HALO_CUTS = (0, 160, 320, 448, ROWS)
+HC = len(HALO_CUTS) - 1
 GC = 4
 GR = BLK // GC
 QUARTER = BLK // 4
@@ -122,19 +123,23 @@
             halo[Y] = jnp.zeros((NC, ROWS, HALF), BF16)
 
     tag = jnp.full((TAG, HALF), seg_ref[0].astype(F32)).astype(BF16)
-    for c in range(NC):
+
+    def mix(c):
         for copy in kv[c]:
             copy.wait()
         halo[X, c, pl.ds(0, BLK)] = (k[c].astype(F32) * v[c].astype(F32)).astype(BF16)
         halo[X, c, pl.ds(BLK, TAG)] = tag
+
+    mix(0)
     pl.semaphore_wait(barrier, 8 - first_z.astype(jnp.int32) - last_z.astype(jnp.int32))
 
-    piece = BLK // HC
-    pieces = [pl.ds(p * piece, piece + (TAG if p == HC - 1 else 0)) for p in range(HC)]
+    pieces = [pl.ds(HALO_CUTS[p], HALO_CUTS[p + 1] - HALO_CUTS[p]) for p in range(HC)]
     z_copies, y_copies, s_copies, s_sems = {}, {}, {}, {}
     gets_y = jnp.logical_or(yh == 1, jnp.logical_not(first_z))
     gives_y = jnp.logical_or(yh == 0, jnp.logical_not(first_z))
     for c in range(NC):
+        if c:
+            mix(c)
         for p, rows in enumerate(pieces):
             z_copies[c, p] = remote(halo.at[X, c, rows], halo.at[Z, c, rows], number(), z_next)
             y_copies[c, p] = [remote(halo.at[src, c, rows], halo.at[Y, c, rows], counter[0], y_far) for src in (X, Z)]
@@ -323,7 +328,6 @@
         give(0, r)
     spectrum(1, X)
     spectrum(1, Z)
-    weights_on(0)
     for p in range(HC):
         y_arrives(1, p)
     pass_on(0, 0)
@@ -342,6 +346,7 @@
     pass_on(0, 3)
     gate(1, 2)
     gate(1, 3)
+    weights_on(0)
 
     own_cols, other_cols = pl.ds(0, BLK), pl.ds(BLK, BLK)
 

time: 53.3 us -> 52.9 us (level)
  no operation moved by 1% of the time
where the time goes in v4:
time: 52.9 us; the launch traced here: 52.7 us
  Pallas kernels  50.2 us (95%)
  local copies, waits for them, and re-layouts  1.87 us (4%)
  between operations  0.66 us (1%)
    pallas_call x1, Pallas kernels, on_device(): pl.pallas_call(kernel, out_shape=jax.ShapeDtypeStruct((BLK, BLK), BF16),...  50.2 us
    unnamed x1, local copies, waits for them, and re-layouts  1.87 us

profile of v4, /device:TPU:128, one launch (start us, length us, event | category | flops | bytes accessed | tf_op | source)
XLA Modules:
  0.0 52.7 jit_solution(5767585342842781709)
XLA Ops:
  0.7 50.2 %hyena.1 = bf16[512,512]{1,0:T(8,128)(2,1)} custom-call(s32[1]{0:T(128)S(6)} %copy.10.seg_ref, bf16[512,512]{1,0:T(8,128)(2,1)} %q_hbm.1, bf16[512,512]{1,0:T(8,128)(2,1)} %k_hbm.1, bf16[512,512]{1,0:T(8,128)(2,1)} %v_hbm.1, bf16[2048,512]{1,0:T(8,128)(2,1)} %filt_hbm.1, bf16[512,4096]{1,0:T(8,128)(2,1)} %w_hbm.1, bf16[1024,512]{1,0:T(8,128)(2,1)} %constant.4.clone.fwd_hbm, ...), custom_call_target="tpu_custom_call" | custom-call | tf_op jit(solution)/shard_map/hyena/pallas_call | solution.py:400
  50.9 1.9 %copy.11 = bf16[512,512]{1,0:T(8,128)(2,1)} copy(bf16[512,512]{1,0:T(8,128)(2,1)} %hyena.1) | data formatting | bytes 1048576

commit v5 on v4

--- a/solution.py
+++ b/solution.py
@@ -18,7 +18,7 @@
 NC = BLK // HALF
 TAG = 16
 ROWS = BLK + TAG
-HALO_CUTS = (0, 160, 320, 448, ROWS)
+HALO_CUTS = (0, 176, 336, 464, ROWS)
 HC = len(HALO_CUTS) - 1
 GC = 4
 GR = BLK // GC

time: 52.9 us -> 53 us (level)
  no operation moved by 1% of the time
where the time goes in v5:
time: 53 us; the launch traced here: 52.9 us
  Pallas kernels  50.4 us (95%)
  local copies, waits for them, and re-layouts  1.87 us (4%)
  between operations  0.66 us (1%)
    pallas_call x1, Pallas kernels, on_device(): pl.pallas_call(kernel, out_shape=jax.ShapeDtypeStruct((BLK, BLK), BF16),...  50.4 us
    unnamed x1, local copies, waits for them, and re-layouts  1.87 us

profile of v5, /device:TPU:128, one launch (start us, length us, event | category | flops | bytes accessed | tf_op | source)
XLA Modules:
  0.0 52.9 jit_solution(15959826222639044402)
XLA Ops:
  0.7 50.4 %hyena.1 = bf16[512,512]{1,0:T(8,128)(2,1)} custom-call(s32[1]{0:T(128)S(6)} %copy.10.seg_ref, bf16[512,512]{1,0:T(8,128)(2,1)} %q_hbm.1, bf16[512,512]{1,0:T(8,128)(2,1)} %k_hbm.1, bf16[512,512]{1,0:T(8,128)(2,1)} %v_hbm.1, bf16[2048,512]{1,0:T(8,128)(2,1)} %filt_hbm.1, bf16[512,4096]{1,0:T(8,128)(2,1)} %w_hbm.1, bf16[1024,512]{1,0:T(8,128)(2,1)} %constant.4.clone.fwd_hbm, ...), custom_call_target="tpu_custom_call" | custom-call | tf_op jit(solution)/shard_map/hyena/pallas_call | solution.py:400
  51.0 1.9 %copy.11 = bf16[512,512]{1,0:T(8,128)(2,1)} copy(bf16[512,512]{1,0:T(8,128)(2,1)} %hyena.1) | data formatting | bytes 1048576
